TPU v7x, 256 devices: a whole 4x4x8 slice. The times are simulated.
256 devices in a mesh: blk: 32 (over z, x), rep: 8 (over y, core).
Axes of the slice: x: 4, y: 4, z: 8, core: 2. Of those that a mesh axis runs over, the one named last changes fastest.
Arguments:
- features: bfloat16 [131072, 256], P(('blk', 'rep')), may hold values from -6 to 6
- weight: bfloat16 [256, 256], replicated, may hold values from -0.375 to 0.375
- tiles: bfloat16 [256, 32, 2, 128, 128], P(('blk', 'rep')), may hold values from -0.1875 to 0.1875
- tile_place: int32 [256, 32, 2], P(('blk', 'rep')), may hold values from 0 to 127
- tile_count: int32 [256, 32], P(('blk', 'rep')), may hold values from 1 to 2, as said below
- cotangent: bfloat16 [131072, 256], P(('blk', 'rep')), may hold values from -6 to 6
Outputs:
- output: bfloat16 [131072, 256], P(('blk', 'rep'))
- grad_features: bfloat16 [131072, 256], P(('blk', 'rep'))
- grad_weight: float32 [256, 256], replicated
Inputs may be any that keep to these rules, and one draw needn't show every extreme that they name: Slots at or beyond tile_count of a device and offset hold no part of the adjacency; one device fills all 2 slots for every offset.
All inputs are finite; a program needn't handle non-finite values.
Results may differ from a plain program's by a relative error of at most 0.018.
Values may be sent and summed in bfloat16 or wider, within the bound.
A program may use at most 128 MiB of HBM per device.

v0:
```python
import math

import jax
import jax.numpy as jnp
from jax import lax
from jax.sharding import PartitionSpec as P


def silu_slope(pre):
    gate = jax.nn.sigmoid(pre)
    return gate * (1.0 + pre * (1.0 - gate))


def body(features, weight, tiles, tile_place, tile_count, cotangent):
    dev_rows, width = features.shape
    block_size = tiles.shape[-1]
    slot_total = tiles.shape[2]
    cycle_size = lax.axis_size("blk")
    share_size = lax.axis_size("rep")
    my_team = lax.axis_index("blk")
    team_rows = dev_rows * share_size
    row_blocks = team_rows // block_size
    col_blocks = dev_rows // block_size
    my_tiles = tiles[0]
    my_place = tile_place[0]
    my_count = tile_count[0]
    slot_ids = jnp.arange(slot_total)

    def forward_team(carry, team_piece, col_team):
        offset = (my_team - col_team) % cycle_size
        team_tiles = my_tiles[offset]
        places = my_place[offset]
        live_count = my_count[offset]
        source = team_piece.reshape(col_blocks, block_size, width)
        taken = source[places % col_blocks]
        product = jnp.einsum("skj,sjf->skf", team_tiles, taken, preferred_element_type=jnp.float32)
        product = jnp.where((slot_ids < live_count)[:, None, None], product, 0.0)
        return carry.at[places // col_blocks].add(product)

    empty = jnp.zeros((row_blocks, block_size, width), jnp.float32)
    piece = lax.all_gather(features, "blk", axis=0, tiled=True)
    team_total = piece.shape[0] // dev_rows

    def one_team(j, acc):
        team_piece = lax.dynamic_slice_in_dim(piece, j * dev_rows, dev_rows, 0)
        return forward_team(acc, team_piece, j)

    partial_value = lax.fori_loop(0, team_total, one_team, empty)
    partial_value = partial_value.reshape(team_rows, width)
    summed = lax.psum_scatter(partial_value, "rep", scatter_dimension=0, tiled=True)
    aggregated = summed.astype(jnp.bfloat16)
    pre = jnp.dot(aggregated, weight, preferred_element_type=jnp.float32)
    out_rows = jax.nn.silu(pre).astype(jnp.bfloat16)
    grad_pre = (cotangent.astype(jnp.float32) * silu_slope(pre)).astype(jnp.bfloat16)
    weight_terms = lax.dot_general(
        aggregated, grad_pre, (((0,), (0,)), ((), ())), preferred_element_type=jnp.float32
    )
    grad_mixed = lax.dot_general(
        grad_pre, weight, (((1,), (1,)), ((), ())), preferred_element_type=jnp.float32
    ).astype(jnp.bfloat16)
    team_grads = lax.all_gather(grad_mixed, "rep", axis=0, tiled=True)
    weight_total = lax.psum(weight_terms, ("blk", "rep"))
    node_total = dev_rows * cycle_size * share_size
    grad_weight = weight_total / math.sqrt(node_total)
    grad_source = team_grads.reshape(row_blocks, block_size, width)

    def backward_team(col_team):
        offset = (my_team - col_team) % cycle_size
        team_tiles = my_tiles[offset]
        places = my_place[offset]
        live_count = my_count[offset]
        result = jnp.zeros((col_blocks, block_size, width), jnp.float32)
        taken = grad_source[places // col_blocks]
        product = jnp.einsum("skj,skf->sjf", team_tiles, taken, preferred_element_type=jnp.float32)
        product = jnp.where((slot_ids < live_count)[:, None, None], product, 0.0)
        result = result.at[places % col_blocks].add(product)
        return result.reshape(dev_rows, width)

    count = dev_rows * lax.axis_size("blk")
    team_ids = jnp.arange(count // dev_rows)
    grad_features = lax.psum_scatter(
        lax.map(backward_team, team_ids).reshape(count, width).astype(jnp.bfloat16),
        "blk",
        scatter_dimension=0,
        tiled=True,
    )
    return (out_rows, grad_features, grad_weight)


def solution(mesh):
    return jax.shard_map(
        body,
        mesh=mesh,
        in_specs=(
            P(("blk", "rep"), None),
            P(),
            P(("blk", "rep"), None, None, None, None),
            P(("blk", "rep"), None, None),
            P(("blk", "rep"), None),
            P(("blk", "rep"), None),
        ),
        out_specs=(P(("blk", "rep"), None), P(("blk", "rep"), None), P()),
        check_vma=False,
    )
```

profile of v0, /device:TPU:8, one launch (start us, length us, event | category | flops | bytes accessed | tf_op | source)
XLA Modules:
  0.0 848.3 jit_solution(7004414944110355993)
XLA Ops:
  8.7 103.1 %all-gather.3.cloned.1.call-done = bf16[16384,256]{1,0:T(8,128)(2,1)} async-done(((bf16[512,256]{1,0:T(8,128)(2,1)}), bf16[16384,256]{1,0:T(8,128)(2,1)}) %all-gather.3.cloned.1.call-update) | async-done | bytes 8388624 | tf_op jit(solution)/shard_map/all_gather | solution.py:41
  111.8 2.5 broadcast_in_dim.78
  114.3 170.6 %while.31 = (s32[]{:T(128)}, f32[32,128,256]{2,1,0:T(8,128)}, s32[]{:T(128)}, s32[32,2]{1,0:T(8,128)S(1)}, s32[32]{0:T(128)S(1)}, /*index=5*/bf16[32,2,128,128]{...) while((s32[]{:T(128)}, f32[32,128,256]{2,1,0:T(8,128)}, ...), condition=%wide.region_2.3_spmd.clone, body=%wide.region_0.2_spmd.clone.sunk | while | flops 16909392 | bytes 2036656 | solution.py:48
  117.3 2.3 scatter_fusion
  122.7 2.3 scatter_fusion
  128.0 2.3 scatter_fusion
  133.3 2.3 scatter_fusion
  138.6 2.3 scatter_fusion
  143.9 2.3 scatter_fusion
  149.3 2.3 scatter_fusion
  154.6 2.3 scatter_fusion
  160.0 2.3 scatter_fusion
  165.3 2.3 scatter_fusion
  170.6 2.3 scatter_fusion
  176.0 2.3 scatter_fusion
  181.3 2.3 scatter_fusion
  186.6 2.3 scatter_fusion
  192.0 2.3 scatter_fusion
  197.3 2.3 scatter_fusion
  202.7 2.3 scatter_fusion
  208.0 2.3 scatter_fusion
  213.3 2.3 scatter_fusion
  218.7 2.3 scatter_fusion
  224.0 2.3 scatter_fusion
  229.3 2.3 scatter_fusion
  234.7 2.3 scatter_fusion
  240.0 2.3 scatter_fusion
  245.3 2.3 scatter_fusion
  250.6 2.3 scatter_fusion
  256.0 2.3 scatter_fusion
  261.3 2.3 scatter_fusion
  266.6 2.3 scatter_fusion
  272.0 2.3 scatter_fusion
  277.3 2.3 scatter_fusion
  282.6 2.3 scatter_fusion
  285.0 34.5 %reduce-scatter.3.cloned.1.call-done = f32[512,256]{1,0:T(8,128)} async-done(((f32[4096,256]{1,0:T(8,128)}), f32[512,256]{1,0:T(8,128)}) %reduce-scatter.3.cloned.1.call-update) | async-done | bytes 524304 | tf_op jit(solution)/shard_map/reduce_scatter | solution.py:50
  319.5 2.2 multiply_convert_fusion
  322.8 2.9 copy.9
  326.7 25.3 %all-gather.5.cloned.1.call-done = bf16[4096,256]{1,0:T(8,128)(2,1)} async-done(((bf16[512,256]{1,0:T(8,128)(2,1)}), bf16[4096,256]{1,0:T(8,128)(2,1)}) %all-gather.5.cloned.1.call-update) | async-done | bytes 2097168 | tf_op jit(solution)/shard_map/all_gather | solution.py:61
  352.0 230.7 %while.32 = (s32[]{:T(128)}, bf16[32,512,256]{2,1,0:T(8,128)(2,1)}, s32[32]{0:T(128)S(1)}, s32[]{:T(128)}, s32[32,2]{1,0:T(8,128)S(1)}, /*index=5*/s32[32]{0:T(1...) while((s32[]{:T(128)}, bf16[32,512,256]{2,1,0:T(8,128)(2,1)}, ...), condition=%wide.region_6.7_spmd.clone, body=%wide.region_4.6_spmd.clone.sunk | while | flops 16909384 | bytes 3085188 | solution.py:82
  374.9 2.2 gather_fusion.1
  389.3 2.2 gather_fusion.1
  403.7 2.2 gather_fusion.1
  411.0 2.2 gather_fusion.1
  447.0 2.2 gather_fusion.1
  562.3 2.2 gather_fusion.1
  582.7 26.8 %all-reduce.2.cloned.1.call-done = f32[256,256]{1,0:T(8,128)} async-done(((f32[256,256]{1,0:T(8,128)}), f32[256,256]{1,0:T(8,128)}) %all-reduce.2.cloned.1.call-update) | async-done | bytes 262160 | tf_op jit(solution)/shard_map/psum | solution.py:62
  611.2 230.6 %reduce-scatter.5.cloned.1.call-done = bf16[512,256]{1,0:T(8,128)(2,1)} async-done(((bf16[16384,256]{1,0:T(8,128)(2,1)}), bf16[512,256]{1,0:T(8,128)(2,1)}) %reduce-scatter.5.cloned.1.call-update) | async-done | bytes 262160 | tf_op jit(solution)/shard_map/reduce_scatter | solution.py:81
  (628 shorter events, 295.1 us)
Async XLA Ops:
  7.2 312.3 %copy-start = (bf16[256,256]{1,0:T(8,128)(2,1)S(1)}, bf16[256,256]{1,0:T(8,128)(2,1)}, u32[]{:S(2)}) copy-start(bf16[256,256]{1,0:T(8,128)(2,1)} %param.11) | copy-start | bytes 393220
  7.2 107.1 %copy-start.4 = (s32[1,32]{1,0:T(1,128)S(1)}, s32[1,32]{1,0:T(1,128)}, u32[]{:S(2)}) copy-start(s32[1,32]{1,0:T(1,128)} %param.14) | copy-start | bytes 388
  7.2 107.1 %copy-start.1 = (bf16[1,32,2,128,128]{4,3,2,1,0:T(8,128)(2,1)S(1)}, bf16[1,32,2,128,128]{4,3,2,1,0:T(8,128)(2,1)}, u32[]{:S(2)}) copy-start(bf16[1,32,2,128,128]{4,3,2,1,0:T(8,128)(2,1)} %param.12) | copy-start | bytes 6291460
  7.2 104.6 %all-gather.3.cloned.1.call-start = ((), (), s32[]{:S(2)}) async-start(), calls=%async_computation.2 | async-start | bytes 8650752 | tf_op jit(solution)/shard_map/all_gather | solution.py:41
  7.9 311.6 %reduce-scatter.3.cloned.1.call-start = ((), (), s32[]{:S(2)}) async-start(), calls=%async_computation.3 | async-start | bytes 4718592 | tf_op jit(solution)/shard_map/reduce_scatter | solution.py:50
  284.9 34.5 %copy-start.3 = (bf16[512,256]{1,0:T(8,128)(2,1)S(1)}, bf16[512,256]{1,0:T(8,128)(2,1)}, u32[]{:S(2)}) copy-start(bf16[512,256]{1,0:T(8,128)(2,1)} %param.15) | copy-start | bytes 786436
  285.0 67.0 %all-gather.5.cloned.1.call-start = ((), (), s32[]{:S(2)}) async-start(), calls=%async_computation.4 | async-start | bytes 2359296 | tf_op jit(solution)/shard_map/all_gather | solution.py:61
  319.5 6.2 copy-start.2
  322.7 286.8 %all-reduce.2.cloned.1.call-start = ((), (), s32[]{:S(2)}) async-start(), calls=%async_computation.6 | async-start | bytes 524288 | tf_op jit(solution)/shard_map/psum | solution.py:62
  326.7 515.2 %reduce-scatter.5.cloned.1.call-start = ((), (), s32[]{:S(2)}) async-start(), calls=%async_computation.5 | async-start | bytes 8650752 | tf_op jit(solution)/shard_map/reduce_scatter | solution.py:81
Sparse Core Ops, SparseCore 0:
  10.6 101.1 all-gather.2
  285.1 34.3 reduce-scatter.2
  322.8 29.1 all-gather.4
  357.9 251.6 all-reduce.1
  614.0 227.8 reduce-scatter.4
where the time goes:
time: 853 us; the launch traced here: 848 us
  waiting for transfers between devices  421 us (49%)
  local copies, waits for them, and re-layouts  205 us (24%)
  other arithmetic  142 us (17%)
  matrix products  42 us (5%)
  loops' own time  24.8 us (3%)
  between operations  13.8 us (2%)
    reduce_scatter x1, waiting for transfers between devices, body(): lax.psum_scatter(lax.map(backward_team, team_ids).reshape(count, width).a...  231 us
    all_gather x1, waiting for transfers between devices, body(): piece = lax.all_gather(features, 'blk', axis=0, tiled=True)  103 us
    scatter-add x32, other arithmetic, forward_team(): return carry.at[places // col_blocks].add(product)  73.9 us
    gather x32, local copies, waits for them, and re-layouts, backward_team(): taken = grad_source[places // col_blocks]  68.7 us
    reduce_scatter x1, waiting for transfers between devices, body(): lax.psum_scatter(partial_value, 'rep', scatter_dimension=0, tiled=True)  34.5 us
    dot_general x32, matrix products, backward_team(): jnp.einsum('skj,skf->sjf', team_tiles, taken, preferred_element_type=jnp....  32.4 us
    dynamic_slice x32, local copies, waits for them, and re-layouts, one_team(): team_piece = lax.dynamic_slice_in_dim(piece, j * dev_rows, dev_rows, 0)  31.1 us
    psum x1, waiting for transfers between devices, body(): weight_total = lax.psum(weight_terms, ('blk', 'rep'))  26.8 us
  transfers between devices with their start and end apart: 5, of which 5 were waited for; matrix products, arithmetic and copies ran while one was open for 25% of the time, Pallas kernels for 0%

commit v1 on v0

v1 whole, which is shorter than its diff:
```python
import functools
import math

import jax
import jax.numpy as jnp
from jax import lax
from jax.experimental import pallas as pl
from jax.experimental.pallas import tpu as pltpu
from jax.sharding import PartitionSpec as P

NZ, NX, NY, NC = 8, 4, 4, 2
BS = 128
F32, BF16 = jnp.float32, jnp.bfloat16
SEM_TOTAL = 220


def rem(a, n):
    return lax.rem(a, jnp.int32(n))


def kernel(
    feat_ref, weight_ref, tiles_ref, code_ref, cot_ref,
    out_ref, gfeat_ref, gweight_ref,
    feats, held0, held1, held2, held3, passing, meta, meta_s, sums, part, sib,
    land_big1, land_big2, land_small1, land_small2,
    agg, grad0, grad1, turned, lhs, rhs, terms, z_out, z_in,
    w_mine, w_z, w_x, w_y, w_c, w_all,
    send_sem, recv_sem, local_sem, meta_sem,
):
    blk, rep = lax.axis_index("blk"), lax.axis_index("rep")
    z, x = lax.div(blk, jnp.int32(NX)), rem(blk, NX)
    y, core = lax.div(rep, jnp.int32(NC)), rem(rep, NC)

    held, grad = (held0, held1, held2, held3), (grad0, grad1)

    def dev(dz=0, dx=0, dy=0, dc=0):
        return {
            "blk": rem(z + dz + NZ, NZ) * NX + rem(x + dx + NX, NX),
            "rep": rem(y + dy + NY, NY) * NC + rem(core + dc, NC),
        }

    peers = [dev(dc=1)]
    peers += [dev(dx=d) for d in range(1, NX)]
    peers += [dev(dy=d) for d in range(1, NY)]
    peers += [dev(dz=d) for d in range(1, NZ)]
    started = []

    def send(src, dst, target):
        n = len(started)
        copy = pltpu.make_async_remote_copy(
            src_ref=src, dst_ref=dst, send_sem=send_sem.at[n], recv_sem=recv_sem.at[n],
            device_id=target, device_id_type=pl.DeviceIdType.MESH,
        )
        copy.start()
        started.append(copy)
        return copy

    own_tiles = pltpu.make_async_copy(tiles_ref.at[:, 0], held[0], local_sem)
    own_tiles.start()

    barrier = pltpu.get_barrier_semaphore()
    for peer in peers:
        pl.semaphore_signal(barrier, inc=1, device_id=peer, device_id_type=pl.DeviceIdType.MESH)

    for q in range(4):
        feats[0, q] = feat_ref[q * BS:(q + 1) * BS, :]

    pl.semaphore_wait(barrier, len(peers))

    gather_r = [send(feats.at[0], feats.at[1], dev(dz=1))]
    gather_l = [send(feats.at[0], feats.at[7], dev(dz=-1))]
    tile_a = send(tiles_ref.at[0:4, 2], passing.at[0], dev(dx=1))
    tile_b = send(tiles_ref.at[4:8, 2], passing.at[1], dev(dx=-1))

    code = code_ref[...]
    ids = lax.broadcasted_iota(jnp.int32, (BS, BS), 0)
    lanes = lax.broadcasted_iota(jnp.int32, (BS, BS), 1)
    flipped = code.T

    def parts_of(value, at):
        inside = at < 64
        live = jnp.logical_and(value >= 128, inside)
        group = jnp.where(inside, (at >> 1) & 3, -1)
        row = jnp.where(live, (value & 127) >> 2, 32)
        return live, group, row, value & 3

    live_e, group_e, row_e, col_e = parts_of(code, ids)
    live_f, group_f, row_f, col_f = parts_of(flipped, lanes)
    key_e, key_f = row_e * 64 + ids, row_f * 64 + lanes
    before = jnp.logical_and(jnp.logical_and(group_e == group_f, lanes < 64), key_f < key_e)

    def count(flags, axis):
        return jnp.sum(jnp.where(flags, 1, 0), axis=axis, keepdims=True)

    rank = count(before, 1)
    same = count(jnp.logical_and(before, row_e == row_f), 1)
    chosen = jnp.logical_and(
        jnp.logical_and(group_e == (lanes >> 4), ids < 64), rank == (lanes & 15)
    )
    entry = (ids >> 3) * 2 + (ids & 1)
    meta[0, 0:1, :] = jnp.sum(jnp.where(chosen, entry, 0), axis=0, keepdims=True)
    meta[0, 1:2, :] = jnp.sum(jnp.where(chosen, col_e, 0), axis=0, keepdims=True)
    meta[0, 2:3, :] = count(jnp.logical_and(chosen, same == 0), 0)
    mine = jnp.logical_and(live_e, group_e == (lanes >> 5))
    here = count(jnp.logical_and(mine, row_e == (lanes & 31)), 0)
    upto = count(jnp.logical_and(mine, row_e <= (lanes & 31)), 0)
    meta[0, 3:4, :] = jnp.where(here > 0, upto - 1, 16)
    meta[0, 4:5, :] = jnp.where(live_f, row_f, 0)[0:1, :]
    meta[0, 5:6, :] = jnp.where(live_f, col_f, 4)[0:1, :]
    meta[0, 6:8, :] = jnp.zeros((2, BS), jnp.int32)
    meta_copies = [send(meta.at[0], meta.at[k], dev(dx=-k)) for k in (1, 2, 3)]
    sums[16] = jnp.zeros((BS, 2 * BS), F32)

    gather_r[0].wait_recv()
    gather_r.append(send(feats.at[1], feats.at[2], dev(dz=1)))
    gather_l[0].wait_recv()
    gather_l.append(send(feats.at[7], feats.at[6], dev(dz=-1)))
    tile_a.wait_recv()
    tile_fa = send(passing.at[0], held[2].at[0:4], dev(dx=1))
    tile_b.wait_recv()
    tile_fb = send(passing.at[1], held[2].at[4:8], dev(dx=-1))
    tile_1 = send(tiles_ref.at[:, 1], held[1], dev(dx=-1))
    tile_3 = send(tiles_ref.at[:, 3], held[3], dev(dx=1))
    gather_r[1].wait_recv()
    gather_r.append(send(feats.at[2], feats.at[3], dev(dz=1)))
    gather_l[1].wait_recv()
    gather_l.append(send(feats.at[6], feats.at[5], dev(dz=-1)))
    for copy in meta_copies:
        copy.wait_recv()
    to_s = pltpu.make_async_copy(meta, meta_s, meta_sem)
    to_s.start()
    gather_r[2].wait_recv()
    half_r = send(feats.at[3, 0:2], feats.at[4, 0:2], dev(dz=1))
    gather_l[2].wait_recv()
    half_l = send(feats.at[5, 2:4], feats.at[4, 2:4], dev(dz=-1))
    to_s.wait()
    own_tiles.wait()
    half_r.wait_recv()
    half_l.wait_recv()

    sib_copies = {}

    def forward(k):
        carry = lax.div(x + k, jnp.int32(NX))

        def four(g, total):
            for u in range(4):
                at = k * 16 + g * 4 + u
                e, col, fresh = meta_s[k, 0, at] & 15, meta_s[k, 1, at] & 3, meta_s[k, 2, at]
                product = jnp.dot(
                    held[k][e >> 1, e & 1], feats[((e >> 1) + carry) & 7, col], preferred_element_type=F32
                )
                total = product + total * (1 - fresh).astype(F32)
                sums[g * 4 + u] = total
            return total

        lax.fori_loop(0, 4, four, jnp.zeros((BS, 2 * BS), F32))

        def place(i, _):
            for cc in range(2):
                for q in range(4):
                    row = (i * 2 + cc) * 4 + q
                    value = sums[jnp.clip(meta_s[k, 3, k * 32 + row], 0, 16)].astype(BF16)
                    part[0, k, i, cc, q] = value[:, :BS]
                    part[1, k, i, cc, q] = value[:, BS:]
            return 0

        lax.fori_loop(0, 4, place, 0)
        for c in range(2):
            sib_copies[c, k] = send(part.at[c, k, :, 1 - core], sib.at[c, k], dev(dc=1))

    forward(0)
    tile_fa.wait_recv()
    tile_fb.wait_recv()
    forward(2)
    tile_1.wait_recv()
    forward(1)
    tile_3.wait_recv()
    forward(3)

    def add(ref, index, *others):
        value = ref[index].astype(F32)
        for other, at in others:
            value = value + other[at].astype(F32)
        return value

    def merge(c, k):
        sib_copies[c, k].wait_recv()

        def one(i, _):
            for q in range(4):
                part[c, k, i, core, q] = add(part, (c, k, i, core, q), (sib, (c, k, i, q))).astype(BF16)
            return 0

        lax.fori_loop(0, NY, one, 0)

    def near(value, step, size):
        return rem(value + step + size, size)

    class Reduce:
        def __init__(self, c, half):
            self.c, self.half = c, half
            self.n = c * 2 + half

        def step(self, d):
            return dev(dx=d) if self.half == 0 else dev(dy=d)

        def cross(self, d):
            return dev(dy=d) if self.half == 0 else dev(dx=d)

        def big(self, away, lo, size):
            q = pl.ds(2 * self.half, 2)
            if self.half == 0:
                return (self.c, away & 3, pl.ds(lo, size), core, q)
            return (self.c, pl.ds(lo, size), near(y, away, NY), core, q)

        def big_block(self, away, at, q):
            if self.half == 0:
                return (self.c, away & 3, at, core, q)
            return (self.c, at, near(y, away, NY), core, 2 + q)

        def small(self, away, q):
            if self.half == 0:
                return (self.c, 0, near(y, away, NY), core, q)
            return (self.c, away & 3, y, core, 2 + q)

        def begin(self):
            n = self.n
            self.r1 = send(part.at[self.big(2, 0, 2)], land_big1.at[n, 0], self.step(1))
            self.l1 = send(part.at[self.big(2, 2, 2)], land_big1.at[n, 1], self.step(-1))
            self.r2 = [send(part.at[self.big(1, 2, 2)], land_big2.at[n, 0, 2:4], self.step(1))]
            self.l2 = [send(part.at[self.big(-1, 0, 2)], land_big2.at[n, 1, 0:2], self.step(-1))]

        def middle(self):
            n = self.n

            def fold(way, lo, away):
                def one(i, _):
                    for q in range(2):
                        at = self.big_block(away, lo + i, q)
                        part[at] = add(part, at, (land_big1, (n, way, i, q))).astype(BF16)
                    return 0

                lax.fori_loop(0, 2, one, 0)

            self.r1.wait_recv()
            fold(0, 0, 1)
            self.r2.append(send(part.at[self.big(1, 0, 2)], land_big2.at[n, 0, 0:2], self.step(1)))
            self.l1.wait_recv()
            fold(1, 2, -1)
            self.l2.append(send(part.at[self.big(-1, 2, 2)], land_big2.at[n, 1, 2:4], self.step(-1)))

        def turn(self):
            n = self.n
            for copy in self.r2 + self.l2:
                copy.wait_recv()

            def one(i, _):
                for q in range(2):
                    at = self.big_block(0, i, q)
                    part[at] = add(part, at, (land_big2, (n, 0, i, q)), (land_big2, (n, 1, i, q))).astype(BF16)
                return 0

            lax.fori_loop(0, 4, one, 0)
            self.r3 = send(part.at[self.small(2, 0)], land_small1.at[n, 0], self.cross(1))
            self.l3 = send(part.at[self.small(2, 1)], land_small1.at[n, 1], self.cross(-1))
            self.r4 = [send(part.at[self.small(1, 1)], land_small2.at[n, 0, 1], self.cross(1))]
            self.l4 = [send(part.at[self.small(-1, 0)], land_small2.at[n, 1, 0], self.cross(-1))]

        def late(self):
            n = self.n
            self.r3.wait_recv()
            at = self.small(1, 0)
            part[at] = add(part, at, (land_small1, (n, 0))).astype(BF16)
            self.r4.append(send(part.at[at], land_small2.at[n, 0, 0], self.cross(1)))
            self.l3.wait_recv()
            at = self.small(-1, 1)
            part[at] = add(part, at, (land_small1, (n, 1))).astype(BF16)
            self.l4.append(send(part.at[at], land_small2.at[n, 1, 1], self.cross(-1)))

        def finish(self):
            n = self.n
            for copy in self.r4 + self.l4:
                copy.wait_recv()
            for q in range(2):
                value = add(part, self.small(0, q), (land_small2, (n, 0, q)), (land_small2, (n, 1, q)))
                row = (2 * self.half + q) * BS
                agg[row:row + BS, self.c * BS:(self.c + 1) * BS] = value.astype(BF16)

    reduces = [[Reduce(c, half) for half in range(2)] for c in range(2)]
    for c in range(2):
        for k in (0, 2, 1, 3):
            merge(c, k)
        for r in reduces[c]:
            r.begin()
    for stage in ("middle", "turn", "late", "finish"):
        for c in range(2):
            for r in reduces[c]:
                getattr(r, stage)()

    pre = jnp.dot(agg[...], weight_ref[...], preferred_element_type=F32)
    gate = jax.nn.sigmoid(pre)
    out_ref[...] = (pre * gate).astype(BF16)
    slope = gate * (1.0 + pre * (1.0 - gate))
    grad_pre = (cot_ref[...].astype(F32) * slope).astype(BF16)
    mixed = lax.dot_general(
        grad_pre, weight_ref[...], (((1,), (1,)), ((), ())), preferred_element_type=F32
    ).astype(BF16)
    for q in range(4):
        for c in range(2):
            grad[c][0, y, core, q] = mixed[q * BS:(q + 1) * BS, c * BS:(c + 1) * BS]

    class Gather:
        def __init__(self, c, half):
            self.c, self.half = c, half
            self.q = pl.ds(2 * half, 2)

        def at(self, first, second, q=None):
            q = self.q if q is None else 2 * self.half + q
            if self.half == 0:
                return (second & 3, near(y, first, NY), core, q)
            return (first & 3, near(y, second, NY), core, q)

        def short(self, d):
            return dev(dy=d) if self.half == 0 else dev(dx=d)

        def long(self, d):
            return dev(dx=d) if self.half == 0 else dev(dy=d)

        def hop(self, first, second, axis, d, q=None):
            there = (first - d, second) if axis == 0 else (first, second - d)
            target = self.short(d) if axis == 0 else self.long(d)
            if self.half == 0:
                there = (first, there[1]) if axis == 1 else (first, second)
            else:
                there = (there[0], second) if axis == 0 else (first, second)
            ref = grad[self.c]
            return send(ref.at[self.at(first, second, q)], ref.at[self.at(*there, q)], target)

        def begin(self):
            self.s = {d: self.hop(0, 0, 0, d) for d in (1, -1)}
            self.g = {(0, d): self.hop(0, 0, 1, d) for d in (1, -1)}

        def spread(self):
            self.s2 = {}
            for d, q in ((1, 0), (-1, 1)):
                self.s[d].wait_recv()
                self.s2[d] = self.hop(-d, 0, 0, d, q)
                for e in (1, -1):
                    self.g[-d, e] = self.hop(-d, 0, 1, e)

        def widen(self):
            for d in (1, -1):
                self.s2[d].wait_recv()
            for e in (1, -1):
                self.g[2, e] = self.hop(2, 0, 1, e)
            self.f = []
            for first in (0, -1):
                self.g[first, 1].wait_recv()
                self.f.append(self.hop(first, -1, 1, 1))

        def relay(self):
            for first in (1, 2):
                self.g[first, -1].wait_recv()
                self.f.append(self.hop(first, 1, 1, -1))
            self.share(0)

        def share(self, second):
            if self.half == 0:
                at = (second & 3, slice(None), core, self.q)
            else:
                at = (slice(None), near(y, second, NY), core, self.q)
            ref = grad[self.c]
            self.shared.append(send(ref.at[at], ref.at[at], dev(dc=1)))

        def close(self):
            for first in (1, 2):
                self.g[first, 1].wait_recv()
            self.share(-1)
            for first in (0, -1):
                self.g[first, -1].wait_recv()
            self.share(1)

        def close2(self):
            for copy in self.f:
                copy.wait_recv()
            self.share(2)

        def settle(self):
            for copy in self.shared:
                copy.wait_recv()

    gathers = [[Gather(c, half) for half in range(2)] for c in range(2)]
    for pair in gathers:
        for g in pair:
            g.shared = []

    def gather_stage(c, stage):
        for g in gathers[c]:
            getattr(g, stage)()

    gather_stage(0, "begin")

    w_terms = lax.dot_general(agg[...], grad_pre, (((0,), (0,)), ((), ())), preferred_element_type=F32)
    for p in range(NZ):
        w_mine[p] = w_terms[p * 32:(p + 1) * 32, :]
    w_z[z] = w_mine[z]
    w_copies = [
        send(w_mine.at[near(z, d, NZ)], w_z.at[z], dev(dz=d)) for d in range(1, NZ)
    ]

    gather_stage(0, "spread")
    gather_stage(1, "begin")
    gather_stage(0, "widen")

    def turn_tiles(n, _):
        for k in range(4):
            for s in range(2):
                turned[k, n, s] = held[k][n, s].T
        return 0

    lax.fori_loop(0, 8, turn_tiles, 0)

    for copy in w_copies:
        copy.wait_recv()
    total = w_z[0]
    for p in range(1, NZ):
        total = total + w_z[p]
    w_x[x] = total
    w_copies = [send(w_x.at[x], w_x.at[x], dev(dx=d)) for d in range(1, NX)]
    gather_stage(0, "relay")
    gather_stage(1, "spread")
    for copy in w_copies:
        copy.wait_recv()
    w_y[y] = (w_x[0] + w_x[1]) + (w_x[2] + w_x[3])
    w_copies = [send(w_y.at[y], w_y.at[y], dev(dy=d)) for d in range(1, NY)]
    gather_stage(0, "close")
    gather_stage(1, "widen")
    for copy in w_copies:
        copy.wait_recv()
    w_c[core] = (w_y[0] + w_y[1]) + (w_y[2] + w_y[3])
    w_copy = send(w_c.at[core], w_c.at[core], dev(dc=1))
    gather_stage(0, "close2")
    gather_stage(1, "relay")
    w_copy.wait_recv()
    w_all[z] = (w_c[0] + w_c[1]) * (1.0 / math.sqrt(NZ * NX * NY * NC * 4 * BS))
    w_copies = [send(w_all.at[z], w_all.at[z], dev(dz=d)) for d in range(1, NZ)]
    gather_stage(0, "settle")

    def backward(c, slot, store):
        for k in range(4):
            m = (slot - lax.div(x + k, jnp.int32(NX))) & 7
            for s in range(2):
                n = k * 2 + s
                at = m * 8 + n
                row, col = meta_s[k, 4, at] & 31, meta_s[k, 5, at]
                tile = turned[k, m, s]
                for q in range(4):
                    lhs[q * BS:(q + 1) * BS, n * BS:(n + 1) * BS] = tile * jnp.where(col == q, 1, 0).astype(BF16)
                rhs[n * BS:(n + 1) * BS, :] = grad[c][k, row >> 3, (row >> 2) & 1, row & 3]
        value = jnp.dot(lhs[...], rhs[...], preferred_element_type=F32)
        for q in range(4):
            store[q] = value[q * BS:(q + 1) * BS, :]

    class Back:
        def __init__(self, c):
            self.c = c

        def begin(self):
            c = self.c
            backward(c, jnp.int32(4), terms.at[0])
            for way in range(2):
                for q in range(2):
                    z_out[c, way, 0, 2 * way + q] = terms[0, 2 * way + q].astype(BF16)
            self.copies = [
                send(z_out.at[c, way, 0, pl.ds(2 * way, 2)], z_in.at[c, way, 0, pl.ds(2 * way, 2)], dev(dz=1 - 2 * way))
                for way in range(2)
            ]

        def step(self, t):
            c = self.c
            away = 4 - t

            def one(way, _):
                backward(c, jnp.where(way == 0, 8 - away, away), terms.at[way])
                return 0

            lax.fori_loop(0, 2, one, 0)
            copies = []
            for way in range(2):
                self.copies[way].wait_recv()
                for q in range(4):
                    value = terms[way, q]
                    if t > 1 or q // 2 == way:
                        value = value + z_in[c, way, t - 1, q].astype(F32)
                    z_out[c, way, t, q] = value.astype(BF16)
                copies.append(send(z_out.at[c, way, t], z_in.at[c, way, t], dev(dz=1 - 2 * way)))
            self.copies = copies

        def finish(self):
            c = self.c
            backward(c, jnp.int32(0), terms.at[0])
            for copy in self.copies:
                copy.wait_recv()
            for q in range(4):
                value = terms[0, q] + z_in[c, 0, 3, q].astype(F32) + z_in[c, 1, 3, q].astype(F32)
                gfeat_ref[q * BS:(q + 1) * BS, c * BS:(c + 1) * BS] = value.astype(BF16)

    backs = [Back(0), Back(1)]
    backs[0].begin()
    gather_stage(1, "close")
    backs[0].step(1)
    gather_stage(1, "close2")
    backs[0].step(2)
    gather_stage(1, "settle")
    backs[1].begin()
    backs[0].step(3)
    backs[1].step(1)
    for copy in w_copies:
        copy.wait_recv()
    for p in range(NZ):
        gweight_ref[p * 32:(p + 1) * 32, :] = w_all[p]
    backs[0].finish()
    backs[1].step(2)
    backs[1].step(3)
    backs[1].finish()
    for copy in started:
        copy.wait_send()


def body(features, weight, tiles, tile_place, tile_count, cotangent):
    rows, width = features.shape
    tiles = tiles.reshape(8, 4, 2, BS, BS)
    live = jnp.arange(2)[None, :] < tile_count[0][:, None]
    code = (tile_place[0] + jnp.where(live, 128, 0)).reshape(64)
    code = jnp.broadcast_to(jnp.concatenate([code, jnp.zeros((64,), jnp.int32)])[:, None], (BS, BS))
    vmem = pl.BlockSpec(memory_space=pltpu.VMEM)
    bf = lambda *lead: pltpu.VMEM(lead + (BS, BS), BF16)
    f32 = lambda *shape: pltpu.VMEM(shape, F32)
    scratch = [
        pltpu.VMEM((8, 4, BS, 2 * BS), BF16),
        bf(8, 2), bf(8, 2), bf(8, 2), bf(8, 2),
        bf(2, 4, 2),
        pltpu.VMEM((4, 8, BS), jnp.int32), pltpu.SMEM((4, 8, BS), jnp.int32),
        f32(17, BS, 2 * BS),
        bf(2, 4, 4, 2, 4), bf(2, 4, 4, 4),
        bf(4, 2, 2, 2), bf(4, 2, 4, 2), bf(4, 2), bf(4, 2, 2),
        pltpu.VMEM((4 * BS, 2 * BS), BF16),
        bf(4, 4, 2, 4), bf(4, 4, 2, 4),
        bf(4, 8, 2),
        pltpu.VMEM((4 * BS, 8 * BS), BF16), pltpu.VMEM((8 * BS, BS), BF16),
        f32(2, 4, BS, BS),
        bf(2, 2, 4, 4), bf(2, 2, 4, 4),
        f32(8, 32, 2 * BS), f32(8, 32, 2 * BS), f32(4, 32, 2 * BS), f32(4, 32, 2 * BS),
        f32(2, 32, 2 * BS), f32(8, 32, 2 * BS),
        pltpu.SemaphoreType.DMA((SEM_TOTAL,)), pltpu.SemaphoreType.DMA((SEM_TOTAL,)),
        pltpu.SemaphoreType.DMA, pltpu.SemaphoreType.DMA,
    ]
    return pl.pallas_call(
        kernel,
        out_shape=(
            jax.ShapeDtypeStruct((rows, width), BF16),
            jax.ShapeDtypeStruct((rows, width), BF16),
            jax.ShapeDtypeStruct((width, width), F32),
        ),
        in_specs=[vmem] * 5,
        out_specs=(vmem,) * 3,
        scratch_shapes=scratch,
        compiler_params=pltpu.CompilerParams(
            collective_id=0, has_side_effects=True, vmem_limit_bytes=56 * 1024 * 1024
        ),
    )(features, weight, tiles, code, cotangent)


def solution(mesh):
    return jax.shard_map(
        body,
        mesh=mesh,
        in_specs=(
            P(("blk", "rep"), None),
            P(),
            P(("blk", "rep"), None, None, None, None),
            P(("blk", "rep"), None, None),
            P(("blk", "rep"), None),
            P(("blk", "rep"), None),
        ),
        out_specs=(P(("blk", "rep"), None), P(("blk", "rep"), None), P()),
        check_vma=False,
    )
```

time: 853 us -> 141 us (0.17)
  waiting for transfers between devices: 421 us -> 0 us
  local copies, waits for them, and re-layouts: 205 us -> 6.69 us
  other arithmetic: 142 us -> 0.73 us
  Pallas kernels: 0 us -> 133 us
  matrix products: 42 us -> 0 us
  loops' own time: 24.8 us -> 0 us
  between operations: 13.8 us -> 0.66 us
    reduce_scatter x2 -> x0, waiting for transfers between devices: 265 us -> none  [the longest x1 231 us: body(): lax.psum_scatter(lax.map(backward_team, team_ids).reshape(count, width).a...]
    pallas_call x0 -> x1, Pallas kernels: none -> 133 us  [body(): pl.pallas_call(kernel, out_shape=(jax.ShapeDtypeStruct((rows, width), BF1...]
    all_gather x2 -> x0, waiting for transfers between devices: 128 us -> none  [the longest x1 103 us: body(): piece = lax.all_gather(features, 'blk', axis=0, tiled=True)]
    scatter-add x64 -> x0, other arithmetic: 96 us -> none  [the longest x32 73.9 us: forward_team(): return carry.at[places // col_blocks].add(product)]
    dynamic_slice x128 -> x0, local copies, waits for them, and re-layouts: 87.4 us -> none  [the longest x32 31.1 us: one_team(): team_piece = lax.dynamic_slice_in_dim(piece, j * dev_rows, dev_rows, 0)]
    gather x64 -> x0, local copies, waits for them, and re-layouts: 86.5 us -> none  [the longest x32 68.7 us: backward_team(): taken = grad_source[places // col_blocks]]
    dot_general x67 -> x0, matrix products: 42 us -> none  [the longest x32 32.4 us: backward_team(): jnp.einsum('skj,skf->sjf', team_tiles, taken, preferred_element_type=jnp....]
    lt x64 -> x0, other arithmetic: 41.5 us -> none  [the longest x32 20.8 us: backward_team(): product = jnp.where((slot_ids < live_count)[:, None, None], product, 0.0)]
  transfers between devices with their start and end apart: 5 -> 0, of which waited for: 5 -> 0; matrix products, arithmetic and copies ran while one was open for 25% -> 0% of each run, Pallas kernels for 0% -> 0%
where the time goes in v1:
time: 141 us
  Pallas kernels  133 us (94%)
  local copies, waits for them, and re-layouts  6.69 us (5%)
    pallas_call x1, Pallas kernels, body(): pl.pallas_call(kernel, out_shape=(jax.ShapeDtypeStruct((rows, width), BF1...  133 us
    unnamed x4, local copies, waits for them, and re-layouts  5.77 us

profile of v1, /device:TPU:8, one launch (start us, length us, event | category | flops | bytes accessed | tf_op | source)
XLA Modules:
  0.0 140.9 jit_solution(10467821204873501674)
XLA Ops:
  0.6 0.8 copy.10
  1.4 0.1 squeeze.3
  1.5 0.7 fusion
  2.2 0.1 select_n.9
  2.4 0.7 broadcast_in_dim.18.code_ref
  3.1 132.8 %shard_map.85 = (bf16[512,256]{1,0:T(8,128)(2,1)}, bf16[512,256]{1,0:T(8,128)(2,1)}, f32[256,256]{1,0:T(8,128)}) custom-call(bf16[512,256]{1,0:T(8,128)(2,1)} %feat_ref.1, bf16[256,256]{1,0:T(8,128)(2,1)} %weight_ref.1, bf16[8,4,2,128,128]{4,3,2,1,0:T(8,128)(2,1)} %bitcast.2, s32[128,128]{1,0:T(8,128)} %broadcast_in_dim.18.code_ref, bf16[512,256]{1,0:T(8,128)(2,1)} %cot_ref.1), custom_call_target="tpu_custom_call" | custom-call | tf_op jit(solution)/shard_map/pallas_call | solution.py:559
  135.9 1.7 %copy.14 = bf16[512,256]{1,0:T(8,128)(2,1)} copy(bf16[512,256]{1,0:T(8,128)(2,1)} %get-tuple-element.6) | data formatting | bytes 524288
  137.5 1.7 %copy.15 = bf16[512,256]{1,0:T(8,128)(2,1)} copy(bf16[512,256]{1,0:T(8,128)(2,1)} %get-tuple-element.7) | data formatting | bytes 524288
  139.2 1.7 %copy.16 = f32[256,256]{1,0:T(8,128)} copy(f32[256,256]{1,0:T(8,128)} %get-tuple-element.8) | data formatting | bytes 524288
  (2 shorter events, 0.0 us)

commit v2 on v1

--- a/solution.py
+++ b/solution.py
@@ -11,7 +11,8 @@
 NZ, NX, NY, NC = 8, 4, 4, 2
 BS = 128
 F32, BF16 = jnp.float32, jnp.bfloat16
-SEM_TOTAL = 220
+SEM_TOTAL = 320
+SPOT = (0, 2, 1, 3)
 
 
 def rem(a, n):
@@ -19,10 +20,10 @@
 
 
 def kernel(
-    feat_ref, weight_ref, tiles_ref, code_ref, cot_ref,
+    feat_ref, weight_ref, tiles_ref, place_ref, count_ref, cot_ref,
     out_ref, gfeat_ref, gweight_ref,
     feats, held0, held1, held2, held3, passing, meta, meta_s, sums, part, sib,
-    land_big1, land_big2, land_small1, land_small2,
+    land_big1, land_big2, land_small,
     agg, grad0, grad1, turned, lhs, rhs, terms, z_out, z_in,
     w_mine, w_z, w_x, w_y, w_c, w_all,
     send_sem, recv_sem, local_sem, meta_sem,
@@ -67,20 +68,36 @@
 
     pl.semaphore_wait(barrier, len(peers))
 
-    gather_r = [send(feats.at[0], feats.at[1], dev(dz=1))]
-    gather_l = [send(feats.at[0], feats.at[7], dev(dz=-1))]
+    around = {}
+
+    def pass_on(step):
+        for half in range(2):
+            rows = pl.ds(2 * half, 2)
+            for way in (1, -1):
+                if step == 3 and half != (way < 0):
+                    continue
+                if step:
+                    around[step - 1, half, way].wait_recv()
+                here, there = (way * step) & 7, (way * (step + 1)) & 7
+                around[step, half, way] = send(feats.at[here, rows], feats.at[there, rows], dev(dz=way))
+
+    pass_on(0)
     tile_a = send(tiles_ref.at[0:4, 2], passing.at[0], dev(dx=1))
     tile_b = send(tiles_ref.at[4:8, 2], passing.at[1], dev(dx=-1))
 
-    code = code_ref[...]
     ids = lax.broadcasted_iota(jnp.int32, (BS, BS), 0)
     lanes = lax.broadcasted_iota(jnp.int32, (BS, BS), 1)
-    flipped = code.T
+    unused = jnp.zeros((1, 64), jnp.int32)
+    places = jnp.concatenate([place_ref[0:1, :], place_ref[1:2, :], unused], axis=1)
+    counts = jnp.concatenate([count_ref[...], count_ref[...], unused], axis=1)
+    places, counts = jnp.broadcast_to(places, (BS, BS)), jnp.broadcast_to(counts, (BS, BS))
+    flipped = places + jnp.where(counts > (lanes >> 5), 128, 0)
+    code = flipped.T
 
     def parts_of(value, at):
         inside = at < 64
         live = jnp.logical_and(value >= 128, inside)
-        group = jnp.where(inside, (at >> 1) & 3, -1)
+        group = jnp.where(inside, at & 3, -1)
         row = jnp.where(live, (value & 127) >> 2, 32)
         return live, group, row, value & 3
 
@@ -97,7 +114,7 @@
     chosen = jnp.logical_and(
         jnp.logical_and(group_e == (lanes >> 4), ids < 64), rank == (lanes & 15)
     )
-    entry = (ids >> 3) * 2 + (ids & 1)
+    entry = ((ids >> 2) & 7) * 2 + (ids >> 5)
     meta[0, 0:1, :] = jnp.sum(jnp.where(chosen, entry, 0), axis=0, keepdims=True)
     meta[0, 1:2, :] = jnp.sum(jnp.where(chosen, col_e, 0), axis=0, keepdims=True)
     meta[0, 2:3, :] = count(jnp.logical_and(chosen, same == 0), 0)
@@ -111,32 +128,33 @@
     meta_copies = [send(meta.at[0], meta.at[k], dev(dx=-k)) for k in (1, 2, 3)]
     sums[16] = jnp.zeros((BS, 2 * BS), F32)
 
-    gather_r[0].wait_recv()
-    gather_r.append(send(feats.at[1], feats.at[2], dev(dz=1)))
-    gather_l[0].wait_recv()
-    gather_l.append(send(feats.at[7], feats.at[6], dev(dz=-1)))
+    pass_on(1)
     tile_a.wait_recv()
     tile_fa = send(passing.at[0], held[2].at[0:4], dev(dx=1))
     tile_b.wait_recv()
     tile_fb = send(passing.at[1], held[2].at[4:8], dev(dx=-1))
     tile_1 = send(tiles_ref.at[:, 1], held[1], dev(dx=-1))
     tile_3 = send(tiles_ref.at[:, 3], held[3], dev(dx=1))
-    gather_r[1].wait_recv()
-    gather_r.append(send(feats.at[2], feats.at[3], dev(dz=1)))
-    gather_l[1].wait_recv()
-    gather_l.append(send(feats.at[6], feats.at[5], dev(dz=-1)))
+    pass_on(2)
     for copy in meta_copies:
         copy.wait_recv()
     to_s = pltpu.make_async_copy(meta, meta_s, meta_sem)
     to_s.start()
-    gather_r[2].wait_recv()
-    half_r = send(feats.at[3, 0:2], feats.at[4, 0:2], dev(dz=1))
-    gather_l[2].wait_recv()
-    half_l = send(feats.at[5, 2:4], feats.at[4, 2:4], dev(dz=-1))
+    own_tiles.wait()
+
+    def turn(k):
+        def one(n, _):
+            for s in range(2):
+                turned[k, n, s] = held[k][n, s].T
+            return 0
+
+        lax.fori_loop(0, 8, one, 0)
+
+    turn(0)
+    pass_on(3)
     to_s.wait()
-    own_tiles.wait()
-    half_r.wait_recv()
-    half_l.wait_recv()
+    for key in ((2, 0, -1), (2, 1, 1), (3, 0, 1), (3, 1, -1)):
+        around[key].wait_recv()
 
     sib_copies = {}
 
@@ -161,22 +179,13 @@
                 for q in range(4):
                     row = (i * 2 + cc) * 4 + q
                     value = sums[jnp.clip(meta_s[k, 3, k * 32 + row], 0, 16)].astype(BF16)
-                    part[0, k, i, cc, q] = value[:, :BS]
-                    part[1, k, i, cc, q] = value[:, BS:]
+                    part[0, SPOT[k], i, cc, q] = value[:, :BS]
+                    part[1, SPOT[k], i, cc, q] = value[:, BS:]
             return 0
 
         lax.fori_loop(0, 4, place, 0)
         for c in range(2):
-            sib_copies[c, k] = send(part.at[c, k, :, 1 - core], sib.at[c, k], dev(dc=1))
-
-    forward(0)
-    tile_fa.wait_recv()
-    tile_fb.wait_recv()
-    forward(2)
-    tile_1.wait_recv()
-    forward(1)
-    tile_3.wait_recv()
-    forward(3)
+            sib_copies[c, k] = send(part.at[c, SPOT[k], :, 1 - core], sib.at[c, SPOT[k]], dev(dc=1))
 
     def add(ref, index, *others):
         value = ref[index].astype(F32)
@@ -186,10 +195,10 @@
 
     def merge(c, k):
         sib_copies[c, k].wait_recv()
+        at = SPOT[k]
 
         def one(i, _):
-            for q in range(4):
-                part[c, k, i, core, q] = add(part, (c, k, i, core, q), (sib, (c, k, i, q))).astype(BF16)
+            part[c, at, i, core] = part[c, at, i, core] + sib[c, at, i]
             return 0
 
         lax.fori_loop(0, NY, one, 0)
@@ -211,25 +220,30 @@
         def big(self, away, lo, size):
             q = pl.ds(2 * self.half, 2)
             if self.half == 0:
-                return (self.c, away & 3, pl.ds(lo, size), core, q)
+                return (self.c, SPOT[away & 3], pl.ds(lo, size), core, q)
             return (self.c, pl.ds(lo, size), near(y, away, NY), core, q)
 
         def big_block(self, away, at, q):
             if self.half == 0:
-                return (self.c, away & 3, at, core, q)
+                return (self.c, SPOT[away & 3], at, core, q)
             return (self.c, at, near(y, away, NY), core, 2 + q)
 
-        def small(self, away, q):
+        def small(self, away, q, whole=False):
             if self.half == 0:
                 return (self.c, 0, near(y, away, NY), core, q)
-            return (self.c, away & 3, y, core, 2 + q)
-
-        def begin(self):
-            n = self.n
-            self.r1 = send(part.at[self.big(2, 0, 2)], land_big1.at[n, 0], self.step(1))
-            self.l1 = send(part.at[self.big(2, 2, 2)], land_big1.at[n, 1], self.step(-1))
-            self.r2 = [send(part.at[self.big(1, 2, 2)], land_big2.at[n, 0, 2:4], self.step(1))]
-            self.l2 = [send(part.at[self.big(-1, 0, 2)], land_big2.at[n, 1, 0:2], self.step(-1))]
+            return (self.c, SPOT[away & 3], y, core, pl.ds(2, 2) if whole else 2 + q)
+
+        def far_r(self):
+            self.r1 = send(part.at[self.big(2, 0, 2)], land_big1.at[self.n, 0], self.step(1))
+
+        def far_l(self):
+            self.l1 = send(part.at[self.big(2, 2, 2)], land_big1.at[self.n, 1], self.step(-1))
+
+        def next_r(self):
+            self.r2 = [send(part.at[self.big(1, 2, 2)], land_big2.at[self.n, 0, 2:4], self.step(1))]
+
+        def next_l(self):
+            self.l2 = [send(part.at[self.big(-1, 0, 2)], land_big2.at[self.n, 1, 0:2], self.step(-1))]
 
         def middle(self):
             n = self.n
@@ -238,7 +252,7 @@
                 def one(i, _):
                     for q in range(2):
                         at = self.big_block(away, lo + i, q)
-                        part[at] = add(part, at, (land_big1, (n, way, i, q))).astype(BF16)
+                        part[at] = part[at] + land_big1[n, way, i, q]
                     return 0
 
                 lax.fori_loop(0, 2, one, 0)
@@ -262,38 +276,47 @@
                 return 0
 
             lax.fori_loop(0, 4, one, 0)
-            self.r3 = send(part.at[self.small(2, 0)], land_small1.at[n, 0], self.cross(1))
-            self.l3 = send(part.at[self.small(2, 1)], land_small1.at[n, 1], self.cross(-1))
-            self.r4 = [send(part.at[self.small(1, 1)], land_small2.at[n, 0, 1], self.cross(1))]
-            self.l4 = [send(part.at[self.small(-1, 0)], land_small2.at[n, 1, 0], self.cross(-1))]
-
-        def late(self):
-            n = self.n
-            self.r3.wait_recv()
-            at = self.small(1, 0)
-            part[at] = add(part, at, (land_small1, (n, 0))).astype(BF16)
-            self.r4.append(send(part.at[at], land_small2.at[n, 0, 0], self.cross(1)))
-            self.l3.wait_recv()
-            at = self.small(-1, 1)
-            part[at] = add(part, at, (land_small1, (n, 1))).astype(BF16)
-            self.l4.append(send(part.at[at], land_small2.at[n, 1, 1], self.cross(-1)))
+            self.last = [
+                send(part.at[self.small(d, pl.ds(0, 2), whole=True)], land_small.at[n, d - 1], self.cross(d))
+                for d in (2, 1, 3)
+            ]
 
         def finish(self):
             n = self.n
-            for copy in self.r4 + self.l4:
+            for copy in self.last:
                 copy.wait_recv()
             for q in range(2):
-                value = add(part, self.small(0, q), (land_small2, (n, 0, q)), (land_small2, (n, 1, q)))
+                value = add(part, self.small(0, q), *[(land_small, (n, d, q)) for d in range(3)])
                 row = (2 * self.half + q) * BS
                 agg[row:row + BS, self.c * BS:(self.c + 1) * BS] = value.astype(BF16)
 
     reduces = [[Reduce(c, half) for half in range(2)] for c in range(2)]
+    forward(0)
+    tile_fa.wait_recv()
+    tile_fb.wait_recv()
+    forward(2)
     for c in range(2):
-        for k in (0, 2, 1, 3):
-            merge(c, k)
-        for r in reduces[c]:
-            r.begin()
-    for stage in ("middle", "turn", "late", "finish"):
+        merge(c, 0)
+        merge(c, 2)
+        reduces[c][1].far_r()
+        reduces[c][0].far_r()
+        reduces[c][0].far_l()
+        reduces[c][1].next_l()
+    tile_1.wait_recv()
+    forward(1)
+    tile_3.wait_recv()
+    forward(3)
+    for c in range(2):
+        merge(c, 1)
+        reduces[c][0].next_r()
+        merge(c, 3)
+        reduces[c][1].far_l()
+        reduces[c][1].next_r()
+        reduces[c][0].next_l()
+    turn(2)
+    turn(1)
+    turn(3)
+    for stage in ("middle", "turn", "finish"):
         for c in range(2):
             for r in reduces[c]:
                 getattr(r, stage)()
@@ -338,28 +361,20 @@
             return send(ref.at[self.at(first, second, q)], ref.at[self.at(*there, q)], target)
 
         def begin(self):
-            self.s = {d: self.hop(0, 0, 0, d) for d in (1, -1)}
+            self.s = {d: self.hop(0, 0, 0, d) for d in (1, -1, 2)}
             self.g = {(0, d): self.hop(0, 0, 1, d) for d in (1, -1)}
 
         def spread(self):
-            self.s2 = {}
-            for d, q in ((1, 0), (-1, 1)):
+            for d in (1, -1, 2):
                 self.s[d].wait_recv()
-                self.s2[d] = self.hop(-d, 0, 0, d, q)
                 for e in (1, -1):
-                    self.g[-d, e] = self.hop(-d, 0, 1, e)
-
-        def widen(self):
-            for d in (1, -1):
-                self.s2[d].wait_recv()
-            for e in (1, -1):
-                self.g[2, e] = self.hop(2, 0, 1, e)
+                    self.g[2 if d == 2 else -d, e] = self.hop(-d, 0, 1, e)
+
+        def relay(self):
             self.f = []
             for first in (0, -1):
                 self.g[first, 1].wait_recv()
                 self.f.append(self.hop(first, -1, 1, 1))
-
-        def relay(self):
             for first in (1, 2):
                 self.g[first, -1].wait_recv()
                 self.f.append(self.hop(first, 1, 1, -1))
@@ -403,7 +418,7 @@
 
     w_terms = lax.dot_general(agg[...], grad_pre, (((0,), (0,)), ((), ())), preferred_element_type=F32)
     for p in range(NZ):
-        w_mine[p] = w_terms[p * 32:(p + 1) * 32, :]
+        w_mine[p] = w_terms[p * 32:(p + 1) * 32, :].astype(BF16)
     w_z[z] = w_mine[z]
     w_copies = [
         send(w_mine.at[near(z, d, NZ)], w_z.at[z], dev(dz=d)) for d in range(1, NZ)
@@ -411,48 +426,30 @@
 
     gather_stage(0, "spread")
     gather_stage(1, "begin")
-    gather_stage(0, "widen")
-
-    def turn_tiles(n, _):
-        for k in range(4):
-            for s in range(2):
-                turned[k, n, s] = held[k][n, s].T
-        return 0
-
-    lax.fori_loop(0, 8, turn_tiles, 0)
-
+    gather_stage(0, "relay")
+    gather_stage(0, "close")
+    gather_stage(1, "spread")
     for copy in w_copies:
         copy.wait_recv()
-    total = w_z[0]
+    total = w_z[0].astype(F32)
     for p in range(1, NZ):
-        total = total + w_z[p]
+        total = total + w_z[p].astype(F32)
     w_x[x] = total
     w_copies = [send(w_x.at[x], w_x.at[x], dev(dx=d)) for d in range(1, NX)]
-    gather_stage(0, "relay")
-    gather_stage(1, "spread")
+    gather_stage(0, "close2")
+    gather_stage(1, "relay")
+    gather_stage(0, "settle")
     for copy in w_copies:
         copy.wait_recv()
     w_y[y] = (w_x[0] + w_x[1]) + (w_x[2] + w_x[3])
     w_copies = [send(w_y.at[y], w_y.at[y], dev(dy=d)) for d in range(1, NY)]
-    gather_stage(0, "close")
-    gather_stage(1, "widen")
-    for copy in w_copies:
-        copy.wait_recv()
-    w_c[core] = (w_y[0] + w_y[1]) + (w_y[2] + w_y[3])
-    w_copy = send(w_c.at[core], w_c.at[core], dev(dc=1))
-    gather_stage(0, "close2")
-    gather_stage(1, "relay")
-    w_copy.wait_recv()
-    w_all[z] = (w_c[0] + w_c[1]) * (1.0 / math.sqrt(NZ * NX * NY * NC * 4 * BS))
-    w_copies = [send(w_all.at[z], w_all.at[z], dev(dz=d)) for d in range(1, NZ)]
-    gather_stage(0, "settle")
 
     def backward(c, slot, store):
         for k in range(4):
             m = (slot - lax.div(x + k, jnp.int32(NX))) & 7
             for s in range(2):
                 n = k * 2 + s
-                at = m * 8 + n
+                at = s * 32 + m * 4 + k
                 row, col = meta_s[k, 4, at] & 31, meta_s[k, 5, at]
                 tile = turned[k, m, s]
                 for q in range(4):
@@ -466,16 +463,17 @@
         def __init__(self, c):
             self.c = c
 
+        def put(self, way, t, q, value):
+            c = self.c
+            z_out[c, way, t, q] = value.astype(BF16)
+            self.copies[way, t, q] = send(z_out.at[c, way, t, q], z_in.at[c, way, t, q], dev(dz=1 - 2 * way))
+
         def begin(self):
-            c = self.c
-            backward(c, jnp.int32(4), terms.at[0])
-            for way in range(2):
-                for q in range(2):
-                    z_out[c, way, 0, 2 * way + q] = terms[0, 2 * way + q].astype(BF16)
-            self.copies = [
-                send(z_out.at[c, way, 0, pl.ds(2 * way, 2)], z_in.at[c, way, 0, pl.ds(2 * way, 2)], dev(dz=1 - 2 * way))
-                for way in range(2)
-            ]
+            self.copies = {}
+            backward(self.c, jnp.int32(4), terms.at[0])
+            for q in range(2):
+                for way in range(2):
+                    self.put(way, 0, 2 * way + q, terms[0, 2 * way + q])
 
         def step(self, t):
             c = self.c
@@ -486,54 +484,63 @@
                 return 0
 
             lax.fori_loop(0, 2, one, 0)
-            copies = []
-            for way in range(2):
-                self.copies[way].wait_recv()
-                for q in range(4):
-                    value = terms[way, q]
-                    if t > 1 or q // 2 == way:
-                        value = value + z_in[c, way, t - 1, q].astype(F32)
-                    z_out[c, way, t, q] = value.astype(BF16)
-                copies.append(send(z_out.at[c, way, t], z_in.at[c, way, t], dev(dz=1 - 2 * way)))
-            self.copies = copies
+            for q in range(4):
+                for way in range(2):
+                    at = (q + 2 * (1 - way)) & 3
+                    value = terms[way, at]
+                    if (way, t - 1, at) in self.copies:
+                        self.copies[way, t - 1, at].wait_recv()
+                        value = value + z_in[c, way, t - 1, at].astype(F32)
+                    self.put(way, t, at, value)
 
         def finish(self):
             c = self.c
             backward(c, jnp.int32(0), terms.at[0])
-            for copy in self.copies:
-                copy.wait_recv()
-            for q in range(4):
-                value = terms[0, q] + z_in[c, 0, 3, q].astype(F32) + z_in[c, 1, 3, q].astype(F32)
+            for n in range(4):
+                q = (n + 2) & 3
+                value = terms[0, q]
+                for way in range(2):
+                    self.copies[way, 3, q].wait_recv()
+                    value = value + z_in[c, way, 3, q].astype(F32)
                 gfeat_ref[q * BS:(q + 1) * BS, c * BS:(c + 1) * BS] = value.astype(BF16)
 
     backs = [Back(0), Back(1)]
     backs[0].begin()
     gather_stage(1, "close")
+    for copy in w_copies:
+        copy.wait_recv()
+    w_c[core] = (w_y[0] + w_y[1]) + (w_y[2] + w_y[3])
+    w_copy = send(w_c.at[core], w_c.at[core], dev(dc=1))
     backs[0].step(1)
     gather_stage(1, "close2")
-    backs[0].step(2)
+    w_copy.wait_recv()
+    w_all[z] = ((w_c[0] + w_c[1]) * (1.0 / math.sqrt(NZ * NX * NY * NC * 4 * BS))).astype(BF16)
+    w_copies = [send(w_all.at[z], w_all.at[z], dev(dz=d)) for d in range(1, NZ)]
     gather_stage(1, "settle")
     backs[1].begin()
+    backs[0].step(2)
+    backs[1].step(1)
     backs[0].step(3)
-    backs[1].step(1)
+    backs[1].step(2)
     for copy in w_copies:
         copy.wait_recv()
     for p in range(NZ):
-        gweight_ref[p * 32:(p + 1) * 32, :] = w_all[p]
+        gweight_ref[p * 32:(p + 1) * 32, :] = w_all[p].astype(F32)
     backs[0].finish()
-    backs[1].step(2)
     backs[1].step(3)
     backs[1].finish()
     for copy in started:
         copy.wait_send()
 
 
+def hand_over(*refs):
+    for source, result in zip(refs[:3], refs[3:]):
+        result[...] = source[...]
+
+
 def body(features, weight, tiles, tile_place, tile_count, cotangent):
     rows, width = features.shape
     tiles = tiles.reshape(8, 4, 2, BS, BS)
-    live = jnp.arange(2)[None, :] < tile_count[0][:, None]
-    code = (tile_place[0] + jnp.where(live, 128, 0)).reshape(64)
-    code = jnp.broadcast_to(jnp.concatenate([code, jnp.zeros((64,), jnp.int32)])[:, None], (BS, BS))
     vmem = pl.BlockSpec(memory_space=pltpu.VMEM)
     bf = lambda *lead: pltpu.VMEM(lead + (BS, BS), BF16)
     f32 = lambda *shape: pltpu.VMEM(shape, F32)
@@ -544,32 +551,37 @@
         pltpu.VMEM((4, 8, BS), jnp.int32), pltpu.SMEM((4, 8, BS), jnp.int32),
         f32(17, BS, 2 * BS),
         bf(2, 4, 4, 2, 4), bf(2, 4, 4, 4),
-        bf(4, 2, 2, 2), bf(4, 2, 4, 2), bf(4, 2), bf(4, 2, 2),
+        bf(4, 2, 2, 2), bf(4, 2, 4, 2), bf(4, 3, 2),
         pltpu.VMEM((4 * BS, 2 * BS), BF16),
         bf(4, 4, 2, 4), bf(4, 4, 2, 4),
         bf(4, 8, 2),
         pltpu.VMEM((4 * BS, 8 * BS), BF16), pltpu.VMEM((8 * BS, BS), BF16),
         f32(2, 4, BS, BS),
         bf(2, 2, 4, 4), bf(2, 2, 4, 4),
-        f32(8, 32, 2 * BS), f32(8, 32, 2 * BS), f32(4, 32, 2 * BS), f32(4, 32, 2 * BS),
-        f32(2, 32, 2 * BS), f32(8, 32, 2 * BS),
+        pltpu.VMEM((8, 32, 2 * BS), BF16), pltpu.VMEM((8, 32, 2 * BS), BF16),
+        f32(4, 32, 2 * BS), f32(4, 32, 2 * BS), f32(2, 32, 2 * BS),
+        pltpu.VMEM((8, 32, 2 * BS), BF16),
         pltpu.SemaphoreType.DMA((SEM_TOTAL,)), pltpu.SemaphoreType.DMA((SEM_TOTAL,)),
         pltpu.SemaphoreType.DMA, pltpu.SemaphoreType.DMA,
     ]
-    return pl.pallas_call(
+    shapes = (
+        jax.ShapeDtypeStruct((rows, width), BF16),
+        jax.ShapeDtypeStruct((rows, width), BF16),
+        jax.ShapeDtypeStruct((width, width), F32),
+    )
+    results = pl.pallas_call(
         kernel,
-        out_shape=(
-            jax.ShapeDtypeStruct((rows, width), BF16),
-            jax.ShapeDtypeStruct((rows, width), BF16),
-            jax.ShapeDtypeStruct((width, width), F32),
-        ),
-        in_specs=[vmem] * 5,
+        out_shape=shapes,
+        in_specs=[vmem] * 6,
         out_specs=(vmem,) * 3,
         scratch_shapes=scratch,
         compiler_params=pltpu.CompilerParams(
             collective_id=0, has_side_effects=True, vmem_limit_bytes=56 * 1024 * 1024
         ),
-    )(features, weight, tiles, code, cotangent)
+    )(features, weight, tiles, tile_place[0].T, tile_count, cotangent)
+    return pl.pallas_call(
+        hand_over, out_shape=shapes, in_specs=[vmem] * 3, out_specs=(vmem,) * 3
+    )(*results)
 
 
 def solution(mesh):

time: 141 us -> 125 us (0.89)
  Pallas kernels: 133 us -> 124 us
  local copies, waits for them, and re-layouts: 6.69 us -> 0 us
    pallas_call x1 -> x2, Pallas kernels: 133 us -> 124 us  [the longest x1 122 us: body(): pl.pallas_call(kernel, out_shape=shapes, in_specs=[vmem] * 6, out_specs=(...]
    unnamed x4 -> x0, local copies, waits for them, and re-layouts: 5.77 us -> none
where the time goes in v2:
time: 125 us; the launch traced here: 124 us
  Pallas kernels  124 us (99%)
    pallas_call x1, Pallas kernels, body(): pl.pallas_call(kernel, out_shape=shapes, in_specs=[vmem] * 6, out_specs=(...  122 us

profile of v2, /device:TPU:8, one launch (start us, length us, event | category | flops | bytes accessed | tf_op | source)
XLA Modules:
  0.0 124.4 jit_solution(17013966991553925876)
XLA Ops:
  0.6 121.8 %shard_map.85 = (bf16[512,256]{1,0:T(8,128)(2,1)}, bf16[512,256]{1,0:T(8,128)(2,1)}, f32[256,256]{1,0:T(8,128)}) custom-call(bf16[512,256]{1,0:T(8,128)(2,1)} %feat_ref.1, bf16[256,256]{1,0:T(8,128)(2,1)} %weight_ref.1, bf16[8,4,2,128,128]{4,3,2,1,0:T(8,128)(2,1)} %bitcast.4, s32[2,32]{1,0:T(2,128)} %bitcast.5, s32[1,32]{1,0:T(1,128)} %count_ref.1, ...), custom_call_target="tpu_custom_call" | custom-call | tf_op jit(solution)/shard_map/pallas_call | solution.py:572
  122.4 2.0 %shard_map.86 = (bf16[512,256]{1,0:T(8,128)(2,1)}, bf16[512,256]{1,0:T(8,128)(2,1)}, f32[256,256]{1,0:T(8,128)}) custom-call(bf16[512,256]{1,0:T(8,128)(2,1)} %get-tuple-element.6.refs_0_, bf16[512,256]{1,0:T(8,128)(2,1)} %get-tuple-element.7.refs_1_, f32[256,256]{1,0:T(8,128)} %get-tuple-element.8.refs_2_), custom_call_target="tpu_custom_call" | custom-call | tf_op jit(solution)/shard_map/pallas_call | solution.py:582

commit v3 on v2

--- a/solution.py
+++ b/solution.py
@@ -25,7 +25,7 @@
     feats, held0, held1, held2, held3, passing, meta, meta_s, sums, part, sib,
     land_big1, land_big2, land_small,
     agg, grad0, grad1, turned, lhs, rhs, terms, z_out, z_in,
-    w_mine, w_z, w_x, w_y, w_c, w_all,
+    w_mine, w_sib, w_half, w_z, w_x, w_y, w_all,
     send_sem, recv_sem, local_sem, meta_sem,
 ):
     blk, rep = lax.axis_index("blk"), lax.axis_index("rep")
@@ -126,7 +126,7 @@
     meta[0, 5:6, :] = jnp.where(live_f, col_f, 4)[0:1, :]
     meta[0, 6:8, :] = jnp.zeros((2, BS), jnp.int32)
     meta_copies = [send(meta.at[0], meta.at[k], dev(dx=-k)) for k in (1, 2, 3)]
-    sums[16] = jnp.zeros((BS, 2 * BS), F32)
+    sums[16] = jnp.zeros((BS, 2 * BS), BF16)
 
     pass_on(1)
     tile_a.wait_recv()
@@ -169,16 +169,18 @@
                     held[k][e >> 1, e & 1], feats[((e >> 1) + carry) & 7, col], preferred_element_type=F32
                 )
                 total = product + total * (1 - fresh).astype(F32)
-                sums[g * 4 + u] = total
+                sums[g * 4 + u] = total.astype(BF16)
             return total
 
-        lax.fori_loop(0, 4, four, jnp.zeros((BS, 2 * BS), F32))
+        total = jnp.zeros((BS, 2 * BS), F32)
+        for g in range(4):
+            total = four(g, total)
 
         def place(i, _):
             for cc in range(2):
                 for q in range(4):
                     row = (i * 2 + cc) * 4 + q
-                    value = sums[jnp.clip(meta_s[k, 3, k * 32 + row], 0, 16)].astype(BF16)
+                    value = sums[jnp.clip(meta_s[k, 3, k * 32 + row], 0, 16)]
                     part[0, SPOT[k], i, cc, q] = value[:, :BS]
                     part[1, SPOT[k], i, cc, q] = value[:, BS:]
             return 0
@@ -313,10 +315,12 @@
         reduces[c][1].far_l()
         reduces[c][1].next_r()
         reduces[c][0].next_l()
-    turn(2)
-    turn(1)
-    turn(3)
-    for stage in ("middle", "turn", "finish"):
+    for c in range(2):
+        for r in reduces[c]:
+            r.middle()
+    for k in (2, 1, 3):
+        turn(k)
+    for stage in ("turn", "finish"):
         for c in range(2):
             for r in reduces[c]:
                 getattr(r, stage)()
@@ -362,6 +366,8 @@
 
         def begin(self):
             self.s = {d: self.hop(0, 0, 0, d) for d in (1, -1, 2)}
+
+        def go(self):
             self.g = {(0, d): self.hop(0, 0, 1, d) for d in (1, -1)}
 
         def spread(self):
@@ -413,18 +419,23 @@
     def gather_stage(c, stage):
         for g in gathers[c]:
             getattr(g, stage)()
+        if stage == "begin":
+            for g in gathers[c]:
+                g.go()
 
     gather_stage(0, "begin")
 
     w_terms = lax.dot_general(agg[...], grad_pre, (((0,), (0,)), ((), ())), preferred_element_type=F32)
+    for p in range(2):
+        w_mine[p] = w_terms[p * BS:(p + 1) * BS, :]
+    w_copy = send(w_mine.at[1 - core], w_sib, dev(dc=1))
+    gather_stage(0, "spread")
+    w_copy.wait_recv()
+    total = w_mine[core] + w_sib[...]
     for p in range(NZ):
-        w_mine[p] = w_terms[p * 32:(p + 1) * 32, :].astype(BF16)
-    w_z[z] = w_mine[z]
-    w_copies = [
-        send(w_mine.at[near(z, d, NZ)], w_z.at[z], dev(dz=d)) for d in range(1, NZ)
-    ]
-
-    gather_stage(0, "spread")
+        w_half[p] = total[p * 16:(p + 1) * 16, :].astype(BF16)
+    w_z[z] = w_half[z]
+    w_copies = [send(w_half.at[near(z, d, NZ)], w_z.at[z], dev(dz=d)) for d in range(1, NZ)]
     gather_stage(1, "begin")
     gather_stage(0, "relay")
     gather_stage(0, "close")
@@ -509,24 +520,26 @@
     gather_stage(1, "close")
     for copy in w_copies:
         copy.wait_recv()
-    w_c[core] = (w_y[0] + w_y[1]) + (w_y[2] + w_y[3])
-    w_copy = send(w_c.at[core], w_c.at[core], dev(dc=1))
+    total = (w_y[0] + w_y[1]) + (w_y[2] + w_y[3])
+    w_all[core, z] = (total * (1.0 / math.sqrt(NZ * NX * NY * NC * 4 * BS))).astype(BF16)
+    w_copies = [send(w_all.at[core, z], w_all.at[core, z], dev(dz=d)) for d in range(1, NZ)]
     backs[0].step(1)
     gather_stage(1, "close2")
-    w_copy.wait_recv()
-    w_all[z] = ((w_c[0] + w_c[1]) * (1.0 / math.sqrt(NZ * NX * NY * NC * 4 * BS))).astype(BF16)
-    w_copies = [send(w_all.at[z], w_all.at[z], dev(dz=d)) for d in range(1, NZ)]
     gather_stage(1, "settle")
     backs[1].begin()
     backs[0].step(2)
     backs[1].step(1)
+    for copy in w_copies:
+        copy.wait_recv()
+    w_copy = send(w_all.at[core], w_all.at[core], dev(dc=1))
     backs[0].step(3)
     backs[1].step(2)
-    for copy in w_copies:
-        copy.wait_recv()
-    for p in range(NZ):
-        gweight_ref[p * 32:(p + 1) * 32, :] = w_all[p].astype(F32)
     backs[0].finish()
+    w_copy.wait_recv()
+    for c in range(2):
+        for p in range(NZ):
+            row = c * BS + p * 16
+            gweight_ref[row:row + 16, :] = w_all[c, p].astype(F32)
     backs[1].step(3)
     backs[1].finish()
     for copy in started:
@@ -549,7 +562,7 @@
         bf(8, 2), bf(8, 2), bf(8, 2), bf(8, 2),
         bf(2, 4, 2),
         pltpu.VMEM((4, 8, BS), jnp.int32), pltpu.SMEM((4, 8, BS), jnp.int32),
-        f32(17, BS, 2 * BS),
+        pltpu.VMEM((17, BS, 2 * BS), BF16),
         bf(2, 4, 4, 2, 4), bf(2, 4, 4, 4),
         bf(4, 2, 2, 2), bf(4, 2, 4, 2), bf(4, 3, 2),
         pltpu.VMEM((4 * BS, 2 * BS), BF16),
@@ -558,9 +571,10 @@
         pltpu.VMEM((4 * BS, 8 * BS), BF16), pltpu.VMEM((8 * BS, BS), BF16),
         f32(2, 4, BS, BS),
         bf(2, 2, 4, 4), bf(2, 2, 4, 4),
-        pltpu.VMEM((8, 32, 2 * BS), BF16), pltpu.VMEM((8, 32, 2 * BS), BF16),
-        f32(4, 32, 2 * BS), f32(4, 32, 2 * BS), f32(2, 32, 2 * BS),
-        pltpu.VMEM((8, 32, 2 * BS), BF16),
+        f32(2, BS, 2 * BS), f32(BS, 2 * BS),
+        pltpu.VMEM((8, 16, 2 * BS), BF16), pltpu.VMEM((8, 16, 2 * BS), BF16),
+        f32(4, 16, 2 * BS), f32(4, 16, 2 * BS),
+        pltpu.VMEM((2, 8, 16, 2 * BS), BF16),
         pltpu.SemaphoreType.DMA((SEM_TOTAL,)), pltpu.SemaphoreType.DMA((SEM_TOTAL,)),
         pltpu.SemaphoreType.DMA, pltpu.SemaphoreType.DMA,
     ]

time: 125 us -> 123 us (0.984)
  Pallas kernels: 124 us -> 121 us
    pallas_call x1, Pallas kernels: 122 us -> 119 us  [body(): pl.pallas_call(kernel, out_shape=shapes, in_specs=[vmem] * 6, out_specs=(...]
where the time goes in v3:
time: 123 us; the launch traced here: 122 us
  Pallas kernels  121 us (98%)
    pallas_call x1, Pallas kernels, body(): pl.pallas_call(kernel, out_shape=shapes, in_specs=[vmem] * 6, out_specs=(...  119 us

profile of v3, /device:TPU:8, one launch (start us, length us, event | category | flops | bytes accessed | tf_op | source)
XLA Modules:
  0.0 121.9 jit_solution(17629653419537836223)
XLA Ops:
  0.6 119.3 %shard_map.85 = (bf16[512,256]{1,0:T(8,128)(2,1)}, bf16[512,256]{1,0:T(8,128)(2,1)}, f32[256,256]{1,0:T(8,128)}) custom-call(bf16[512,256]{1,0:T(8,128)(2,1)} %feat_ref.1, bf16[256,256]{1,0:T(8,128)(2,1)} %weight_ref.1, bf16[8,4,2,128,128]{4,3,2,1,0:T(8,128)(2,1)} %bitcast.4, s32[2,32]{1,0:T(2,128)} %bitcast.5, s32[1,32]{1,0:T(1,128)} %count_ref.1, ...), custom_call_target="tpu_custom_call" | custom-call | tf_op jit(solution)/shard_map/pallas_call | solution.py:586
  119.9 2.0 %shard_map.86 = (bf16[512,256]{1,0:T(8,128)(2,1)}, bf16[512,256]{1,0:T(8,128)(2,1)}, f32[256,256]{1,0:T(8,128)}) custom-call(bf16[512,256]{1,0:T(8,128)(2,1)} %get-tuple-element.6.refs_0_, bf16[512,256]{1,0:T(8,128)(2,1)} %get-tuple-element.7.refs_1_, f32[256,256]{1,0:T(8,128)} %get-tuple-element.8.refs_2_), custom_call_target="tpu_custom_call" | custom-call | tf_op jit(solution)/shard_map/pallas_call | solution.py:596

commit v4 on v3

--- a/solution.py
+++ b/solution.py
@@ -440,6 +440,9 @@
     gather_stage(0, "relay")
     gather_stage(0, "close")
     gather_stage(1, "spread")
+    gather_stage(0, "close2")
+    gather_stage(1, "relay")
+    gather_stage(0, "settle")
     for copy in w_copies:
         copy.wait_recv()
     total = w_z[0].astype(F32)
@@ -447,13 +450,6 @@
         total = total + w_z[p].astype(F32)
     w_x[x] = total
     w_copies = [send(w_x.at[x], w_x.at[x], dev(dx=d)) for d in range(1, NX)]
-    gather_stage(0, "close2")
-    gather_stage(1, "relay")
-    gather_stage(0, "settle")
-    for copy in w_copies:
-        copy.wait_recv()
-    w_y[y] = (w_x[0] + w_x[1]) + (w_x[2] + w_x[3])
-    w_copies = [send(w_y.at[y], w_y.at[y], dev(dy=d)) for d in range(1, NY)]
 
     def backward(c, slot, store):
         for k in range(4):
@@ -518,29 +514,33 @@
     backs = [Back(0), Back(1)]
     backs[0].begin()
     gather_stage(1, "close")
+    backs[0].step(1)
+    gather_stage(1, "close2")
+    for copy in w_copies:
+        copy.wait_recv()
+    w_y[y] = (w_x[0] + w_x[1]) + (w_x[2] + w_x[3])
+    w_copies = [send(w_y.at[y], w_y.at[y], dev(dy=d)) for d in range(1, NY)]
+    gather_stage(1, "settle")
+    backs[1].begin()
+    backs[0].step(2)
     for copy in w_copies:
         copy.wait_recv()
     total = (w_y[0] + w_y[1]) + (w_y[2] + w_y[3])
     w_all[core, z] = (total * (1.0 / math.sqrt(NZ * NX * NY * NC * 4 * BS))).astype(BF16)
     w_copies = [send(w_all.at[core, z], w_all.at[core, z], dev(dz=d)) for d in range(1, NZ)]
-    backs[0].step(1)
-    gather_stage(1, "close2")
-    gather_stage(1, "settle")
-    backs[1].begin()
-    backs[0].step(2)
     backs[1].step(1)
+    backs[0].step(3)
+    backs[1].step(2)
     for copy in w_copies:
         copy.wait_recv()
     w_copy = send(w_all.at[core], w_all.at[core], dev(dc=1))
-    backs[0].step(3)
-    backs[1].step(2)
     backs[0].finish()
+    backs[1].step(3)
     w_copy.wait_recv()
     for c in range(2):
         for p in range(NZ):
             row = c * BS + p * 16
             gweight_ref[row:row + 16, :] = w_all[c, p].astype(F32)
-    backs[1].step(3)
     backs[1].finish()
     for copy in started:
         copy.wait_send()
@@ -586,7 +586,7 @@
     results = pl.pallas_call(
         kernel,
         out_shape=shapes,
-        in_specs=[vmem] * 6,
+        in_specs=[vmem, vmem, pl.BlockSpec(memory_space=pl.ANY), vmem, vmem, vmem],
         out_specs=(vmem,) * 3,
         scratch_shapes=scratch,
         compiler_params=pltpu.CompilerParams(

time: 123 us -> 121 us (0.984)
    pallas_call x1, Pallas kernels: 119 us -> 118 us  [body(): pl.pallas_call(kernel, out_shape=shapes, in_specs=[vmem, vmem, pl.BlockSp...]
where the time goes in v4:
time: 121 us
  Pallas kernels  120 us (99%)
    pallas_call x1, Pallas kernels, body(): pl.pallas_call(kernel, out_shape=shapes, in_specs=[vmem, vmem, pl.BlockSp...  118 us

profile of v4, /device:TPU:8, one launch (start us, length us, event | category | flops | bytes accessed | tf_op | source)
XLA Modules:
  0.0 120.5 jit_solution(15356836496031863172)
XLA Ops:
  0.6 117.9 %shard_map.85 = (bf16[512,256]{1,0:T(8,128)(2,1)}, bf16[512,256]{1,0:T(8,128)(2,1)}, f32[256,256]{1,0:T(8,128)}) custom-call(bf16[512,256]{1,0:T(8,128)(2,1)} %feat_ref.1, bf16[256,256]{1,0:T(8,128)(2,1)} %weight_ref.1, bf16[8,4,2,128,128]{4,3,2,1,0:T(8,128)(2,1)} %bitcast.4, s32[2,32]{1,0:T(2,128)} %bitcast.5, s32[1,32]{1,0:T(1,128)} %count_ref.1, ...), custom_call_target="tpu_custom_call" | custom-call | tf_op jit(solution)/shard_map/pallas_call | solution.py:586
  118.5 2.0 %shard_map.86 = (bf16[512,256]{1,0:T(8,128)(2,1)}, bf16[512,256]{1,0:T(8,128)(2,1)}, f32[256,256]{1,0:T(8,128)}) custom-call(bf16[512,256]{1,0:T(8,128)(2,1)} %get-tuple-element.6.refs_0_, bf16[512,256]{1,0:T(8,128)(2,1)} %get-tuple-element.7.refs_1_, f32[256,256]{1,0:T(8,128)} %get-tuple-element.8.refs_2_), custom_call_target="tpu_custom_call" | custom-call | tf_op jit(solution)/shard_map/pallas_call | solution.py:596
